TPU v7x, 512 devices: a whole 4x4x16 slice. The times are simulated.
512 devices in a mesh: blk: 16 (over x_hi, y, core), dom: 32 (over z, x_lo).
Axes of the slice: x: 4 (x_hi: 2, x_lo: 2; x = x_hi * 2 + x_lo), y: 4, z: 16, core: 2. Of those that a mesh axis runs over, the one named last changes fastest.
Arguments:
- features: bfloat16 [32, 8192, 256], P('dom', 'blk'), may hold values from -6 to 6
- weight: bfloat16 [256, 256], replicated, may hold values from -0.375 to 0.375
- tiles: bfloat16 [32, 16, 16, 6, 128, 128], P('dom', 'blk'), may hold values from -0.15234375 to 0.15234375
- tile_pos: int32 [32, 16, 16, 6], P('dom', 'blk'), may hold values from 0 to 15, as said below
- tile_count: int32 [32, 16, 16], P('dom', 'blk'), may hold values from 1 to 6
- send_list: int32 [32, 16, 32, 32], P('dom', 'blk'), may hold values from 0 to 511
- send_count: int32 [32, 16, 32], P('dom', 'blk'), may hold values from 0 to 32, as said below
- owner_map: int32 [32, 16, 32, 32], P('dom', 'blk'), may hold values from 0 to 511
- halo_weight: float32 [32, 16, 32, 32], P('dom', 'blk'), may hold values from 0.25 to 1
- cotangent: bfloat16 [32, 8192, 256], P('dom', 'blk'), may hold values from -6 to 6
Outputs:
- layer_out: bfloat16 [32, 8192, 256], P('dom', 'blk')
- feature_grad: bfloat16 [32, 8192, 256], P('dom', 'blk')
- weight_grad: float32 [256, 256], replicated
Inputs may be any that keep to these rules, and one draw needn't show every extreme that they name: `tile_pos`: the 6 positions of one row group in one column group are distinct. `send_count`: zero where the peer is the sender's own partition.
All inputs are finite; a program needn't handle non-finite values.
Results may differ from a plain program's by a relative error of at most 0.019.
Values may be sent and summed in bfloat16 or wider, within the bound.
A program may use at most 128 MiB of HBM per device.

v0:
```python
import jax
import jax.numpy as jnp
from jax import lax
from jax.sharding import PartitionSpec as P


def spread_rows(tile_set, positions, counts, panel, per):
    groups, slots = positions.shape
    tile = tile_set.shape[-1]
    width = panel.shape[-1]
    grid = panel.reshape(groups, per, tile, width)
    column = positions % per
    row_tile = positions // per
    picked = grid[jnp.arange(groups)[:, None], column]
    product = jnp.einsum("gtij,gtjf->gtif", tile_set, picked, preferred_element_type=jnp.float32)
    live = jnp.arange(slots)[None, :] < counts[:, None]
    select = ((row_tile[..., None] == jnp.arange(per)[None, None, :]) & live[..., None]).astype(
        jnp.float32
    )
    return jnp.einsum("gtif,gtr->rif", product, select).reshape(per * tile, width)


def spread_cols(tile_set, positions, counts, grad_rows, per):
    groups, slots = positions.shape
    tile = tile_set.shape[-1]
    width = grad_rows.shape[-1]
    grid = grad_rows.reshape(per, tile, width)
    column = positions % per
    row_tile = positions // per
    picked = grid[row_tile]
    product = jnp.einsum("gtij,gtif->gtjf", tile_set, picked, preferred_element_type=jnp.float32)
    live = jnp.arange(slots)[None, :] < counts[:, None]
    select = ((column[..., None] == jnp.arange(per)[None, None, :]) & live[..., None]).astype(
        jnp.float32
    )
    return jnp.einsum("gtjf,gtc->gcjf", product, select).reshape(groups * per * tile, width)


def on_device(
    features,
    weight,
    tiles,
    tile_pos,
    tile_count,
    send_list,
    send_count,
    owner_map,
    halo_weight,
    cotangent,
):
    feats = features[0]
    rows, width = feats.shape
    tile_set = tiles[0, 0]
    positions = tile_pos[0, 0]
    counts = tile_count[0, 0]
    tile = tile_set.shape[-1]
    per = rows // tile
    send_rows = send_list[0, 0]
    send_live = send_count[0, 0]
    owners = owner_map[0, 0]
    edge_weight = halo_weight[0, 0]
    grad_in = cotangent[0]
    slots = send_rows.shape[1]
    live = (jnp.arange(slots)[None, :] < send_live[:, None])[..., None]
    empty = jnp.zeros((rows, width), jnp.float32)
    projected = jnp.dot(feats, weight, preferred_element_type=jnp.float32).astype(jnp.bfloat16)
    part_tiles = tile_set
    part_pos = positions
    part_count = counts
    local = spread_rows(
        part_tiles, part_pos, part_count, lax.all_gather(projected, "blk", axis=0, tiled=True), per
    )
    outgoing = jnp.where(live, projected[send_rows], jnp.zeros((), jnp.bfloat16))
    incoming = lax.all_to_all(outgoing, "dom", split_axis=0, concat_axis=0, tiled=True)
    weighted = edge_weight.reshape(-1, 1) * incoming.reshape(-1, width).astype(jnp.float32)
    halo_sum = empty.at[owners.reshape(-1)].add(weighted)
    layer_out = (local + halo_sum).astype(jnp.bfloat16)
    back = (edge_weight[..., None] * grad_in[owners].astype(jnp.float32)).astype(jnp.bfloat16)
    returned = lax.all_to_all(back, "dom", split_axis=0, concat_axis=0, tiled=True)
    returned = jnp.where(live, returned, jnp.zeros((), jnp.bfloat16))
    halo_back = empty.at[send_rows.reshape(-1)].add(returned.reshape(-1, width).astype(jnp.float32))
    part_tiles = tile_set
    part_pos = positions
    part_count = counts
    local_grad = lax.psum_scatter(
        spread_cols(part_tiles, part_pos, part_count, grad_in, per).astype(jnp.bfloat16),
        "blk",
        scatter_dimension=0,
        tiled=True,
    ).astype(jnp.float32)
    proj_grad = (local_grad + halo_back).astype(jnp.bfloat16)
    feature_grad = lax.dot_general(
        proj_grad, weight, (((1,), (1,)), ((), ())), preferred_element_type=jnp.float32
    )
    feature_grad = feature_grad.astype(jnp.bfloat16)
    weight_term = lax.dot_general(
        feats, proj_grad, (((0,), (0,)), ((), ())), preferred_element_type=jnp.float32
    )
    total = lax.psum(weight_term, ("blk", "dom"))
    scale = float(lax.axis_size("blk") * lax.axis_size("dom") * rows) ** (-0.5)
    return (layer_out[None], feature_grad[None], total * scale)


def solution(mesh):
    return jax.shard_map(
        on_device,
        mesh=mesh,
        in_specs=(
            P("dom", "blk", None),
            P(),
            P("dom", "blk", None, None, None, None),
            P("dom", "blk", None, None),
            P("dom", "blk", None),
            P("dom", "blk", None, None),
            P("dom", "blk", None),
            P("dom", "blk", None, None),
            P("dom", "blk", None, None),
            P("dom", "blk", None),
        ),
        out_specs=(P("dom", "blk", None), P("dom", "blk", None), P()),
        check_vma=False,
    )
```

profile of v0, /device:TPU:1, one launch (start us, length us, event | category | flops | bytes accessed | tf_op | source)
XLA Modules:
  0.0 745.7 jit_solution(18372749111417586942)
XLA Ops:
  10.1 6.9 gather_fusion.2
  17.0 7.3 fusion.7
  24.3 11.7 %copy.29 = bf16[16,6,256,128]{2,1,3,0:T(8,128)(2,1)} copy(bf16[16,6,256,128]{3,2,1,0:T(8,128)(2,1)} %fusion.7) | data formatting | bytes 12582912 | tf_op jit(solution)/shard_map/gtij,gtif->gtjf/dot_general | solution.py:31
  36.2 5.7 fusion.4
  41.9 2.8 copy.25
  46.2 5.0 gather_fusion.3
  51.1 2.0 fusion.17
  53.2 17.1 %all-to-all-start.1 = ((bf16[32,32,256]{2,1,0:T(8,128)(2,1)}), bf16[32,32,256]{2,1,0:T(8,128)(2,1)}, u32[]{:S(2)}, u32[]{:S(2)}) async-start(bf16[32,32,256]{2,1,0:T(8,128)(2,1)} %fusion.17), calls=%async_computation.2 | async-start | bytes 1048576 | tf_op jit(solution)/shard_map/all_to_all | solution.py:79
  73.2 5.0 gather_fusion.1
  79.5 21.8 %all-to-all-done.1 = bf16[32,32,256]{2,1,0:T(8,128)(2,1)} async-done(((bf16[32,32,256]{2,1,0:T(8,128)(2,1)}), bf16[32,32,256]{2,1,0:T(8,128)(2,1)}, u32[]{:S(2)}, u32[]{:S(2)}) %all-to-all-start.1) | async-done | bytes 524320 | tf_op jit(solution)/shard_map/all_to_all | solution.py:79
  101.3 2.4 broadcast_select_fusion
  103.7 48.8 %reduce-scatter.2.cloned.1.call-done = bf16[512,256]{1,0:T(8,128)(2,1)} async-done(((bf16[8192,256]{1,0:T(8,128)(2,1)}), bf16[512,256]{1,0:T(8,128)(2,1)}) %reduce-scatter.2.cloned.1.call-update) | async-done | bytes 262160 | tf_op jit(solution)/shard_map/reduce_scatter | solution.py:85
  152.5 1.8 convert_element_type.47
  154.3 8.3 %scatter_custom_fusion.1 = f32[512,256]{1,0:T(8,128)} fusion(f32[512,256]{1,0:T(8,128)} %convert_element_type.47, s32[1024]{0:T(1024)} %bitcast.130, bf16[1024,256]{1,0:T(8,128)(2,1)} %bitcast.127), kind=kCustom, calls=%fused_computation.20 | custom fusion | flops 524288 | bytes 1048576 | tf_op jit(solution)/shard_map/scatter-add | solution.py:81
  162.6 2.1 convolution_bitcast_fusion
  167.0 12.4 %all-to-all-start = ((bf16[32,32,256]{2,1,0:T(8,128)(2,1)}), bf16[32,32,256]{2,1,0:T(8,128)(2,1)}, u32[]{:S(2)}, u32[]{:S(2)}) async-start(bf16[32,32,256]{2,1,0:T(8,128)(2,1)} %get-tuple-element.12), calls=%async_computation | async-start | bytes 1048576 | tf_op jit(solution)/shard_map/all_to_all | solution.py:74
  179.9 2.0 fusion.14
  181.9 444.9 %all-reduce.2.cloned.1.call-done = f32[256,256]{0,1:T(8,128)} async-done(((f32[256,256]{0,1:T(8,128)}), f32[256,256]{0,1:T(8,128)}) %all-reduce.2.cloned.1.call-update) | async-done | bytes 262160 | tf_op jit(solution)/shard_map/psum | solution.py:99
  628.6 70.2 %all-gather.2.cloned.1.call-done = bf16[8192,256]{1,0:T(8,128)(2,1)} async-done(((bf16[512,256]{1,0:T(8,128)(2,1)}), bf16[8192,256]{1,0:T(8,128)(2,1)}) %all-gather.2.cloned.1.call-update) | async-done | bytes 4194320 | tf_op jit(solution)/shard_map/all_gather | solution.py:71
  698.8 8.8 %gather_fusion = bf16[96,128,256]{2,1,0:T(8,128)(2,1)} fusion(bf16[16,4,128,256]{3,2,1,0:T(8,128)(2,1)} %bitcast.123, s32[96]{0:T(128)S(1)} %reshape.324), kind=kCustom, calls=%fused_computation | custom fusion | bytes 12583680 | tf_op jit(solution)/shard_map/gather | solution.py:14
  707.7 7.3 fusion.9
  714.9 9.1 %copy.27 = bf16[16,6,256,128]{2,0,1,3:T(8,128)(2,1)} copy(bf16[16,6,256,128]{3,2,1,0:T(8,128)(2,1)} %fusion.9) | data formatting | bytes 12582912 | tf_op jit(solution)/shard_map/gtij,gtjf->gtif/dot_general | solution.py:15
  724.0 3.8 fusion.11
  728.7 8.7 %scatter_custom_fusion = f32[512,256]{1,0:T(8,128)} fusion(f32[512,256]{1,0:T(8,128)} %bitcast.126, s32[1024]{0:T(1024)S(1)} %bitcast.129, bf16[1024,256]{1,0:T(8,128)(2,1)} %bitcast.31, f32[1024]{0:T(1024)S(1)} %mul.26), kind=kCustom, calls=%fused_computation.25 | custom fusion | flops 786432 | bytes 1052672 | tf_op jit(solution)/shard_map/scatter-add | solution.py:76
  (57 shorter events, 15.9 us)
Async XLA Ops:
  7.2 9.9 %copy-start = (bf16[1,1,16,6,128,128]{5,4,3,2,1,0:T(8,128)(2,1)S(1)}, bf16[1,1,16,6,128,128]{5,4,3,2,1,0:T(8,128)(2,1)}, u32[]{:S(2)}) copy-start(bf16[1,1,16,6,128,128]{5,4,3,2,1,0:T(8,128)(2,1)} %param.12) | copy-start | bytes 9437188
  7.2 145.3 %reduce-scatter.2.cloned.1.call-start = ((), (), s32[]{:S(2)}) async-start(), calls=%async_computation.4 | async-start | bytes 4456448 | tf_op jit(solution)/shard_map/reduce_scatter | solution.py:85
  24.3 11.8 %copy-start.9 = (s32[1,1,16]{2,1,0:T(1,128)S(1)}, s32[1,1,16]{2,1,0:T(1,128)}, u32[]{:S(2)}) copy-start(s32[1,1,16]{2,1,0:T(1,128)} %param.14) | copy-start | bytes 196
  36.2 5.7 copy-start.5
  41.9 2.8 copy-start.4
  41.9 4.2 copy-start.1
  44.7 27.2 %copy-start.3 = (bf16[256,256]{1,0:T(8,128)(2,1)S(1)}, bf16[256,256]{1,0:T(8,128)(2,1)}, u32[]{:S(2)}) copy-start(bf16[256,256]{1,0:T(8,128)(2,1)} %param.11) | copy-start | bytes 393220
  53.2 48.1 %all-to-all-start.1 = ((bf16[32,32,256]{2,1,0:T(8,128)(2,1)}), bf16[32,32,256]{2,1,0:T(8,128)(2,1)}, u32[]{:S(2)}, u32[]{:S(2)}) async-start(bf16[32,32,256]{2,1,0:T(8,128)(2,1)} %fusion.17), calls=%async_computation.2 | async-start | bytes 1048576 | tf_op jit(solution)/shard_map/all_to_all | solution.py:79
  70.3 109.3 %copy-start.7 = (s32[16,6]{0,1:T(8,128)S(1)}, s32[16,6]{0,1:T(8,128)}, u32[]{:S(2)}) copy-start(s32[16,6]{0,1:T(8,128)} %get-tuple-element.14) | copy-start | bytes 1156
  70.3 109.4 %copy-start.6 = (pred[16,6]{1,0:T(8,128)(4,1)S(1)}, pred[16,6]{1,0:T(8,128)(4,1)}, u32[]{:S(2)}) copy-start(pred[16,6]{1,0:T(8,128)(4,1)} %copy-done.5) | copy-start | bytes 292
  70.3 556.5 %all-reduce.2.cloned.1.call-start = ((), (), s32[]{:S(2)}) async-start(), calls=%async_computation.5 | async-start | bytes 524288 | tf_op jit(solution)/shard_map/psum | solution.py:99
  73.2 91.5 %copy-start.2 = (bf16[512,256]{1,0:T(8,128)(2,1)}, bf16[512,256]{1,0:T(8,128)(2,1)S(1)}, u32[]{:S(2)}) copy-start(bf16[512,256]{1,0:T(8,128)(2,1)S(1)} %convolution_convert_fusion.1) | copy-start | bytes 786436
  79.5 99.9 %copy-start.8 = (s32[16,6,1]{0,2,1:T(1,128)S(1)}, s32[16,6,1]{0,2,1:T(1,128)}, u32[]{:S(2)}) copy-start(s32[16,6,1]{0,2,1:T(1,128)} %get-tuple-element.10) | copy-start | bytes 1156
  164.7 534.2 %all-gather.2.cloned.1.call-start = ((), (), s32[]{:S(2)}) async-start(), calls=%async_computation.3 | async-start | bytes 4456448 | tf_op jit(solution)/shard_map/all_gather | solution.py:71
  167.0 561.7 %all-to-all-start = ((bf16[32,32,256]{2,1,0:T(8,128)(2,1)}), bf16[32,32,256]{2,1,0:T(8,128)(2,1)}, u32[]{:S(2)}, u32[]{:S(2)}) async-start(bf16[32,32,256]{2,1,0:T(8,128)(2,1)} %get-tuple-element.12), calls=%async_computation | async-start | bytes 1048576 | tf_op jit(solution)/shard_map/all_to_all | solution.py:74
Sparse Core Ops, SparseCore 0:
  44.9 107.5 reduce-scatter.1
  164.8 461.9 all-reduce.1
  630.7 68.0 all-gather.1
where the time goes:
time: 747 us; the launch traced here: 746 us
  waiting for transfers between devices  586 us (78%)
  local copies, waits for them, and re-layouts  54.8 us (7%)
  other arithmetic  31.5 us (4%)
  starting transfers between devices  29.6 us (4%)
  matrix products  29.3 us (4%)
  between operations  13.9 us (2%)
    psum x1, waiting for transfers between devices, on_device(): total = lax.psum(weight_term, ('blk', 'dom'))  445 us
    all_gather x1, waiting for transfers between devices, on_device(): lax.all_gather(projected, 'blk', axis=0, tiled=True)  70.2 us
    reduce_scatter x1, waiting for transfers between devices, on_device(): lax.psum_scatter(spread_cols(part_tiles, part_pos, part_count, grad_in, p...  48.8 us
    all_to_all x1, waiting for transfers between devices, on_device(): lax.all_to_all(back, 'dom', split_axis=0, concat_axis=0, tiled=True)  21.8 us
    all_to_all x1, starting transfers between devices, on_device(): lax.all_to_all(back, 'dom', split_axis=0, concat_axis=0, tiled=True)  17.1 us
  transfers between devices with their start and end apart: 5, of which 4 were waited for; matrix products, arithmetic and copies ran while one was open for 7% of the time, Pallas kernels for 0%

commit v1 on v0

v1 whole, which is shorter than its diff:
```python
import functools

import jax
import jax.numpy as jnp
from jax import lax
from jax.experimental import pallas as pl
from jax.experimental.pallas import tpu as pltpu
from jax.sharding import PartitionSpec as P

MESH = pl.DeviceIdType.MESH
NB = 16
ND = 32
CHIPS = NB // 2
TILE = 128
PER = 4
ROWS = TILE * PER
TPG = 6
F = 256
SLOTS = 32
LIST = ND * SLOTS
PIECE = F // NB
NEAR = 8
FAR = ND // NEAR
MIB = 1 << 20

bf16 = jnp.bfloat16
f32 = jnp.float32


def dot(a, b, ca=1, cb=0):
    return lax.dot_general(a, b, (((ca,), (cb,)), ((), ())), preferred_element_type=f32)


def local_kernel(
    pos_ref,
    count_ref,
    tiles_ref,
    feats_ref,
    weight_ref,
    cot_ref,
    send_ref,
    owner_ref,
    hw_ref,
    adj_ref,
    partial_ref,
    proj_ref,
    out_ref,
    back_ref,
    pick_ref,
    high_ref,
    low_ref,
):
    c = pl.program_id(0)

    @pl.when(c == 0)
    def _():
        projected = dot(feats_ref[...], weight_ref[...]).astype(bf16)
        proj_ref[...] = projected

        def build(i, carry):
            at = pl.ds(pl.multiple_of(i * TILE, TILE), TILE)
            row = lax.broadcasted_iota(jnp.int32, (TILE, LIST), 0) + i * TILE
            pick_ref[at, :] = jnp.where(row == send_ref[...], 1.0, 0.0).astype(bf16)
            hw = hw_ref[...]
            high = hw.astype(bf16).astype(f32)
            mine = row == owner_ref[...]
            high_ref[at, :] = jnp.where(mine, high, 0.0).astype(bf16)
            low_ref[at, :] = jnp.where(mine, hw - high, 0.0).astype(bf16)
            return carry

        lax.fori_loop(0, PER, build, 0)
        out_ref[...] = dot(pick_ref[...], projected, 0, 0).astype(bf16)
        cot = cot_ref[...]
        back = dot(high_ref[...], cot, 0, 0) + dot(low_ref[...], cot, 0, 0)
        back_ref[...] = back.astype(bf16)

    adj_ref[...] = jnp.zeros_like(adj_ref)
    for t in range(TPG):

        @pl.when(t < count_ref[c])
        def _():
            pos = pos_ref[c * TPG + t]
            r = pl.multiple_of(pos // PER * TILE, TILE)
            k = pl.multiple_of(pos % PER * TILE, TILE)
            adj_ref[0, pl.ds(r, TILE), pl.ds(k, TILE)] = tiles_ref[0, t]

    partial_ref[0, 0] = dot(adj_ref[0], cot_ref[...], 0, 0).astype(bf16)


def local_part(pos, count, tiles, feats, weight, cot, send, owner, hw):
    whole = lambda *shape: pl.BlockSpec(shape, lambda c, *_: (0,) * len(shape))
    shape = jax.ShapeDtypeStruct
    return pl.pallas_call(
        local_kernel,
        grid_spec=pltpu.PrefetchScalarGridSpec(
            num_scalar_prefetch=2,
            grid=(NB,),
            in_specs=[
                pl.BlockSpec((1, TPG, TILE, TILE), lambda c, *_: (c, 0, 0, 0)),
                whole(ROWS, F),
                whole(F, F),
                whole(ROWS, F),
                whole(1, LIST),
                whole(1, LIST),
                whole(1, LIST),
            ],
            out_specs=[
                pl.BlockSpec((1, ROWS, ROWS), lambda c, *_: (c, 0, 0)),
                pl.BlockSpec((1, 1, ROWS, F), lambda c, *_: (c % 2, c // 2, 0, 0)),
                whole(ROWS, F),
                whole(LIST, F),
                whole(LIST, F),
                whole(ROWS, LIST),
                whole(ROWS, LIST),
                whole(ROWS, LIST),
            ],
        ),
        out_shape=[
            shape((NB, ROWS, ROWS), bf16),
            shape((2, CHIPS, ROWS, F), bf16),
            shape((ROWS, F), bf16),
            shape((LIST, F), bf16),
            shape((LIST, F), bf16),
            shape((ROWS, LIST), bf16),
            shape((ROWS, LIST), bf16),
            shape((ROWS, LIST), bf16),
        ],
        compiler_params=pltpu.CompilerParams(vmem_limit_bytes=40 * MIB),
    )(pos, count, tiles, feats, weight, cot, send, owner, hw)


def mesh_kernel(
    adj_hbm,
    partial_hbm,
    out_hbm,
    back_hbm,
    pick_hbm,
    high_hbm,
    low_hbm,
    proj_ref,
    feats_ref,
    weight_ref,
    layer_ref,
    fgrad_ref,
    wgrad_ref,
    adj,
    own,
    pick,
    high,
    low,
    pair_got,
    pair_sum,
    rs_got,
    returned,
    incoming,
    gathered,
    acc,
    term,
    chunk_a,
    chunk_b,
    chunk_c,
    got_a,
    got_b,
    got_c,
    total,
    load_sem,
    pair_send,
    pair_recv,
    rs_send,
    rs_recv,
    back_send,
    back_recv,
    out_send,
    out_recv,
    ag_send,
    ag_recv,
    sib_send,
    sib_recv,
    ar_send,
    ar_recv,
):
    b = lax.axis_index("blk")
    d = lax.axis_index("dom")
    core = lax.rem(b, 2)
    chip = b // 2
    sibling = b + 1 - 2 * core

    def remote(src, dst, send, recv, blk, dom):
        return pltpu.make_async_remote_copy(
            src_ref=src,
            dst_ref=dst,
            send_sem=send,
            recv_sem=recv,
            device_id=(blk, dom),
            device_id_type=MESH,
        )

    def await_bytes(ref, sem):
        pltpu.make_async_copy(ref, ref, sem).wait()

    def loop(lo, hi, body):
        def step(i, carry):
            body(i)
            return carry

        lax.fori_loop(lo, hi, step, 0)

    def block(i, n):
        return pl.ds(pl.multiple_of(i * n, n), n)

    loads = [
        pltpu.make_async_copy(src, dst, load_sem.at[i])
        for i, (src, dst) in enumerate(
            (
                (partial_hbm.at[core], own),
                (pick_hbm, pick),
                (adj_hbm, adj),
                (high_hbm, high),
                (low_hbm, low),
            )
        )
    ]
    for load in loads:
        load.start()

    barrier = pltpu.get_barrier_semaphore()

    def greet_dom(k):
        pl.semaphore_signal(
            barrier, inc=1, device_id=(b, lax.rem(d + k, ND)), device_id_type=MESH
        )

    def greet_blk(k):
        pl.semaphore_signal(
            barrier, inc=1, device_id=(lax.rem(b + k, NB), d), device_id_type=MESH
        )

    loop(1, ND, greet_dom)
    loop(1, NB, greet_blk)
    pl.semaphore_wait(barrier, ND + NB - 2)

    def pair_copy(j):
        at = lax.rem(chip + j, CHIPS)
        return remote(
            partial_hbm.at[1 - core, at],
            pair_got.at[at],
            pair_send,
            pair_recv.at[j],
            sibling,
            d,
        )

    loop(1, CHIPS + 1, lambda j: pair_copy(j).start())

    def dom_send(src, dst, send, recv):
        def body(i):
            half = i // 2
            k = half + 1 + lax.rem(i, 2) * (ND - 2 - 2 * half)
            q = lax.rem(d + k, ND)
            remote(
                src.at[block(q, SLOTS)], dst.at[block(d, SLOTS)], send, recv, b, q
            ).start()

        loop(0, ND - 1, body)

    dom_send(back_hbm, returned, back_send, back_recv)

    loads[0].wait()

    def rs_copy(j):
        at = lax.rem(chip + j, CHIPS)
        return remote(
            pair_sum.at[j], rs_got.at[j], rs_send, rs_recv.at[j], 2 * at + core, d
        )

    def pair_step(j):
        at = lax.rem(chip + j, CHIPS)
        pair_copy(j).wait_recv()
        both = own[at].astype(f32) + pair_got[at].astype(f32)
        pair_sum[j] = both.astype(bf16)
        rs_copy(j).start()

    loop(1, CHIPS, pair_step)

    def ag_copy(j):
        to = 2 * lax.rem(chip + j, CHIPS) + core
        return remote(proj_ref, gathered.at[b], ag_send, ag_recv.at[j], to, d)

    def sib_copy(j):
        at = 2 * lax.rem(chip + CHIPS - j, CHIPS) + core
        return remote(
            gathered.at[at], gathered.at[at], sib_send, sib_recv.at[j], sibling, d
        )

    loop(1, CHIPS, lambda j: ag_copy(j).start())
    remote(proj_ref, gathered.at[b], sib_send, sib_recv.at[0], sibling, d).start()
    dom_send(out_hbm, incoming, out_send, out_recv)

    pair_copy(CHIPS).wait_recv()
    acc[...] = own[chip].astype(f32) + pair_got[chip].astype(f32)
    zero = jnp.zeros((SLOTS, F), bf16)
    returned[block(d, SLOTS), :] = zero
    incoming[block(d, SLOTS), :] = zero

    def rs_step(j):
        rs_copy(j).wait_recv()
        acc[...] += rs_got[j].astype(f32)

    loop(1, CHIPS, rs_step)
    others = pl.ds(0, LIST - SLOTS)
    await_bytes(returned.at[others], back_recv)
    loads[1].wait()
    grad = (acc[...] + dot(pick[...], returned[...])).astype(bf16)
    term[...] = dot(feats_ref[...], grad, 0, 0)

    def blk_send(src_of, dst_of, stage):
        def body(k):
            to = lax.rem(b + k, NB)
            remote(
                src_of(to), dst_of(k), ar_send.at[stage], ar_recv.at[stage], to, d
            ).start()

        loop(1, NB, body)

    blk_send(lambda to: term.at[block(to, PIECE)], lambda k: got_a.at[k], 0)
    fgrad_ref[...] = dot(grad, weight_ref[...], 1, 1).astype(bf16)
    loads[2].wait()

    acc[...] = dot(adj[b], proj_ref[...])

    def ag_step(j):
        at = 2 * lax.rem(chip + CHIPS - j, CHIPS) + core
        ag_copy(j).wait_recv()
        sib_copy(j).start()
        acc[...] += dot(adj[at], gathered[at])

    loop(1, CHIPS, ag_step)

    def sib_step(j):
        at = 2 * lax.rem(chip + CHIPS - j, CHIPS) + 1 - core
        sib_copy(j).wait_recv()
        acc[...] += dot(adj[at], gathered[at])

    await_bytes(got_a.at[pl.ds(1, NB - 1)], ar_recv.at[0])
    piece = term[block(b, PIECE), :]
    for k in range(1, NB):
        piece = piece + got_a[k]
    chunk_a[...] = piece

    def near_send(k):
        to = d // NEAR * NEAR + lax.rem(lax.rem(d, NEAR) + k, NEAR)
        remote(chunk_a, got_b.at[k], ar_send.at[1], ar_recv.at[1], b, to).start()

    loop(1, NEAR, near_send)
    loop(0, 4, sib_step)
    await_bytes(got_b.at[pl.ds(1, NEAR - 1)], ar_recv.at[1])
    piece = chunk_a[...]
    for k in range(1, NEAR):
        piece = piece + got_b[k]
    chunk_b[...] = piece

    def far_send(k):
        to = lax.rem(d + k * NEAR, ND)
        remote(chunk_b, got_c.at[k], ar_send.at[2], ar_recv.at[2], b, to).start()

    loop(1, FAR, far_send)
    loop(4, CHIPS, sib_step)
    await_bytes(got_c.at[pl.ds(1, FAR - 1)], ar_recv.at[2])
    piece = chunk_b[...]
    for k in range(1, FAR):
        piece = piece + got_c[k]
    piece = piece * (float(NB * ND * ROWS) ** -0.5)
    chunk_c[...] = piece
    blk_send(lambda to: chunk_c, lambda k: total.at[block(b, PIECE)], 3)
    total[block(b, PIECE), :] = piece

    loads[3].wait()
    loads[4].wait()
    await_bytes(incoming.at[others], out_recv)
    came = incoming[...]
    halo = dot(high[...], came) + dot(low[...], came)
    layer_ref[...] = (acc[...] + halo).astype(bf16)
    await_bytes(total.at[pl.ds(0, F - PIECE)], ar_recv.at[3])
    wgrad_ref[...] = total[...]

    await_bytes(pair_got, pair_send)
    await_bytes(rs_got.at[pl.ds(1, CHIPS - 1)], rs_send)
    await_bytes(returned.at[others], back_send)
    await_bytes(incoming.at[others], out_send)
    await_bytes(rs_got.at[pl.ds(1, CHIPS - 1)], ag_send)
    await_bytes(rs_got, sib_send)
    await_bytes(got_a.at[pl.ds(1, NB - 1)], ar_send.at[0])
    await_bytes(got_b.at[pl.ds(1, NEAR - 1)], ar_send.at[1])
    await_bytes(got_c.at[pl.ds(1, FAR - 1)], ar_send.at[2])
    await_bytes(got_a.at[pl.ds(1, NB - 1)], ar_send.at[3])


def mesh_part(adj, partial, out, back, pick, high, low, proj, feats, weight):
    shape = jax.ShapeDtypeStruct
    far = pl.BlockSpec(memory_space=pl.ANY)
    near = pl.BlockSpec(memory_space=pltpu.VMEM)
    dma = pltpu.SemaphoreType.DMA
    vmem = pltpu.VMEM
    return pl.pallas_call(
        mesh_kernel,
        out_shape=[
            shape((ROWS, F), bf16),
            shape((ROWS, F), bf16),
            shape((F, F), f32),
        ],
        in_specs=[far] * 7 + [near] * 3,
        out_specs=[near] * 3,
        scratch_shapes=[
            vmem((NB, ROWS, ROWS), bf16),
            vmem((CHIPS, ROWS, F), bf16),
            vmem((ROWS, LIST), bf16),
            vmem((ROWS, LIST), bf16),
            vmem((ROWS, LIST), bf16),
            vmem((CHIPS, ROWS, F), bf16),
            vmem((CHIPS, ROWS, F), bf16),
            vmem((CHIPS, ROWS, F), bf16),
            vmem((LIST, F), bf16),
            vmem((LIST, F), bf16),
            vmem((NB, ROWS, F), bf16),
            vmem((ROWS, F), f32),
            vmem((F, F), f32),
            vmem((PIECE, F), f32),
            vmem((PIECE, F), f32),
            vmem((PIECE, F), f32),
            vmem((NB, PIECE, F), f32),
            vmem((NEAR, PIECE, F), f32),
            vmem((FAR, PIECE, F), f32),
            vmem((F, F), f32),
            dma((5,)),
            dma,
            dma((CHIPS + 1,)),
            dma,
            dma((CHIPS,)),
            dma,
            dma,
            dma,
            dma,
            dma,
            dma((CHIPS,)),
            dma,
            dma((CHIPS,)),
            dma((4,)),
            dma((4,)),
        ],
        compiler_params=pltpu.CompilerParams(
            collective_id=0, has_side_effects=True, vmem_limit_bytes=48 * MIB
        ),
    )(adj, partial, out, back, pick, high, low, proj, feats, weight)


def on_device(
    features,
    weight,
    tiles,
    tile_pos,
    tile_count,
    send_list,
    send_count,
    owner_map,
    halo_weight,
    cotangent,
):
    live = jnp.arange(SLOTS)[None, :] < send_count[0, 0][:, None]
    send = jnp.where(live, send_list[0, 0], -1).reshape(1, LIST)
    adj, partial, proj, out, back, pick, high, low = local_part(
        tile_pos.reshape(-1),
        tile_count.reshape(-1),
        tiles[0, 0],
        features[0],
        weight,
        cotangent[0],
        send,
        owner_map.reshape(1, LIST),
        halo_weight.reshape(1, LIST),
    )
    layer_out, feature_grad, weight_grad = mesh_part(
        adj, partial, out, back, pick, high, low, proj, features[0], weight
    )
    return (layer_out[None], feature_grad[None], weight_grad)


def solution(mesh):
    return jax.shard_map(
        on_device,
        mesh=mesh,
        in_specs=(
            P("dom", "blk", None),
            P(),
            P("dom", "blk", None, None, None, None),
            P("dom", "blk", None, None),
            P("dom", "blk", None),
            P("dom", "blk", None, None),
            P("dom", "blk", None),
            P("dom", "blk", None, None),
            P("dom", "blk", None, None),
            P("dom", "blk", None),
        ),
        out_specs=(P("dom", "blk", None), P("dom", "blk", None), P()),
        check_vma=False,
    )
```

time: 747 us -> 138 us (0.18)
  waiting for transfers between devices: 586 us -> 0 us
  Pallas kernels: 0 us -> 122 us
  local copies, waits for them, and re-layouts: 54.8 us -> 14.6 us
  other arithmetic: 31.5 us -> 0.74 us
  starting transfers between devices: 29.6 us -> 0 us
  matrix products: 29.3 us -> 0 us
  between operations: 13.9 us -> 0.66 us
    psum x1 -> x0, waiting for transfers between devices: 445 us -> none  [on_device(): total = lax.psum(weight_term, ('blk', 'dom'))]
    pallas_call x0 -> x2, Pallas kernels: none -> 122 us  [the longest x1 110 us: mesh_part(): pl.pallas_call(mesh_kernel, out_shape=[shape((ROWS, F), bf16), shape((ROW...]
    all_gather x1 -> x0, waiting for transfers between devices: 70.2 us -> none  [on_device(): lax.all_gather(projected, 'blk', axis=0, tiled=True)]
    reduce_scatter x1 -> x0, waiting for transfers between devices: 48.8 us -> none  [on_device(): lax.psum_scatter(spread_cols(part_tiles, part_pos, part_count, grad_in, p...]
    all_to_all x2 -> x0, starting transfers between devices: 29.5 us -> none  [the longest x1 17.1 us: on_device(): lax.all_to_all(back, 'dom', split_axis=0, concat_axis=0, tiled=True)]
    dot_general x7 -> x0, matrix products: 29.3 us -> none  [the longest x1 7.32 us: spread_cols(): jnp.einsum('gtij,gtif->gtjf', tile_set, picked, preferred_element_type=jn...]
    gather x4 -> x0, local copies, waits for them, and re-layouts: 25.6 us -> none  [the longest x1 8.8 us: spread_rows(): picked = grid[jnp.arange(groups)[:, None], column]]
    all_to_all x2 -> x0, waiting for transfers between devices: 21.8 us -> none  [the longest x1 21.8 us: on_device(): lax.all_to_all(back, 'dom', split_axis=0, concat_axis=0, tiled=True)]
  transfers between devices with their start and end apart: 5 -> 0, of which waited for: 4 -> 0; matrix products, arithmetic and copies ran while one was open for 7% -> 0% of each run, Pallas kernels for 0% -> 0%
where the time goes in v1:
time: 138 us
  Pallas kernels  122 us (88%)
  local copies, waits for them, and re-layouts  14.6 us (11%)
    pallas_call x1, Pallas kernels, mesh_part(): pl.pallas_call(mesh_kernel, out_shape=[shape((ROWS, F), bf16), shape((ROW...  110 us
    unnamed x20, local copies, waits for them, and re-layouts  12 us
    pallas_call x1, Pallas kernels, local_part(): pl.pallas_call(local_kernel, grid_spec=pltpu.PrefetchScalarGridSpec(num_s...  11.2 us

profile of v1, /device:TPU:1, one launch (start us, length us, event | category | flops | bytes accessed | tf_op | source)
XLA Modules:
  0.0 137.7 jit_solution(10456615930257559730)
XLA Ops:
  0.6 0.8 squeeze.16
  1.4 0.7 iota_compare_fusion
  2.2 0.1 lt.29
  2.3 0.8 reshape.54.owner_ref
  3.1 0.8 reshape.55.hw_ref
  3.9 0.8 copy.14
  4.6 0.1 reshape.52.pos_ref
  4.7 0.0 copy-start.1
  4.7 1.9 %copy-done.1 = bf16[1,1,16,6,128,128]{5,4,3,2,1,0:T(8,128)(2,1)S(1)} copy-done((bf16[1,1,16,6,128,128]{5,4,3,2,1,0:T(8,128)(2,1)S(1)}, bf16[1,1,16,6,128,128]{5,4,3,2,1,0:T(8,128)(2,1)}, u32[]{:S(2)}) %copy-start.1) | copy-done | bytes 3145752
  6.6 0.0 copy-start.2
  6.6 0.9 copy-done.2
  7.6 0.0 copy-start.4
  7.6 0.9 copy-done.4
  8.5 0.0 copy-start.6
  8.5 0.9 copy-done.6
  9.4 0.7 copy-done.7
  10.1 11.2 %shard_map.121 = (bf16[16,512,512]{2,1,0:T(8,128)(2,1)}, bf16[2,8,512,256]{3,2,1,0:T(8,128)(2,1)S(1)}, bf16[512,256]{1,0:T(8,128)(2,1)S(1)}, bf16[1024,256]{1,0:...) custom-call(s32[96]{0:T(128)S(1)} %reshape.52.pos_ref, ...), custom_call_target="tpu_custom_call" | custom-call | tf_op jit(solution)/shard_map/pallas_call | solution.py:93
  21.3 2.0 %copy-done = bf16[2,8,512,256]{3,2,1,0:T(8,128)(2,1)} copy-done((bf16[2,8,512,256]{3,2,1,0:T(8,128)(2,1)}, bf16[2,8,512,256]{3,2,1,0:T(8,128)(2,1)S(1)}, u32[]{:S(2)}) %copy-start) | copy-done | bytes 4194328
  23.3 0.9 copy-done.3
  24.2 0.9 copy-done.5
  25.1 110.4 %shard_map.122 = (bf16[512,256]{1,0:T(8,128)(2,1)S(1)}, bf16[512,256]{1,0:T(8,128)(2,1)S(1)}, f32[256,256]{1,0:T(8,128)S(1)}) custom-call(bf16[16,512,512]{2,1,0:T(8,128)(2,1)} %get-tuple-element.14.adj_hbm, bf16[2,8,512,256]{3,2,1,0:T(8,128)(2,1)} %copy-done, bf16[1024,256]{1,0:T(8,128)(2,1)S(1)} %get-tuple-element.16.out_hbm, ...), custom_call_target="tpu_custom_call" | custom-call | tf_op jit(solution)/shard_map/pallas_call | solution.py:404
  135.6 0.7 copy.18
  136.3 0.7 copy.19
  137.0 0.7 copy.20
  (5 shorter events, 0.0 us)
Async XLA Ops:
  4.7 1.9 %copy-start.1 = (bf16[1,1,16,6,128,128]{5,4,3,2,1,0:T(8,128)(2,1)S(1)}, bf16[1,1,16,6,128,128]{5,4,3,2,1,0:T(8,128)(2,1)}, u32[]{:S(2)}) copy-start(bf16[1,1,16,6,128,128]{5,4,3,2,1,0:T(8,128)(2,1)} %param.12) | copy-start | bytes 9437188
  6.6 0.9 copy-start.2
  7.6 0.9 copy-start.4
  8.5 0.9 copy-start.6
  9.4 0.7 copy-start.7
  21.3 2.0 %copy-start = (bf16[2,8,512,256]{3,2,1,0:T(8,128)(2,1)}, bf16[2,8,512,256]{3,2,1,0:T(8,128)(2,1)S(1)}, u32[]{:S(2)}) copy-start(bf16[2,8,512,256]{3,2,1,0:T(8,128)(2,1)S(1)} %get-tuple-element.15.partial_hbm) | copy-start | bytes 12582916
  23.3 0.9 copy-start.3
  24.2 0.9 copy-start.5

commit v2 on v1

v2 whole, which is shorter than its diff:
```python
import functools

import jax
import jax.numpy as jnp
from jax import lax
from jax.experimental import pallas as pl
from jax.experimental.pallas import tpu as pltpu
from jax.sharding import PartitionSpec as P

MESH = pl.DeviceIdType.MESH
NB = 16
ND = 32
CHIPS = NB // 2
COL = 4
HALF = 256
TILE = 128
PER = 4
ROWS = TILE * PER
TPG = 6
F = 256
SLOTS = 32
LIST = ND * SLOTS
PIECE = F // NB
NEAR = 8
FAR = ND // NEAR
MIB = 1 << 20

bf16 = jnp.bfloat16
f32 = jnp.float32


def dot(a, b, ca=1, cb=0):
    return lax.dot_general(a, b, (((ca,), (cb,)), ((), ())), preferred_element_type=f32)


def mesh_kernel(
    pos_ref,
    count_ref,
    tiles_hbm,
    feats_hbm,
    cot_hbm,
    weight_hbm,
    send_hbm,
    live_hbm,
    owner_hbm,
    hw_hbm,
    layer_ref,
    fgrad_ref,
    wgrad_ref,
    tiles,
    feats,
    cot,
    weight,
    send_rows,
    owner_rows,
    hw_rows,
    live_row,
    adj,
    pick,
    high,
    low,
    outgoing,
    back,
    returned,
    incoming,
    other,
    own,
    pair_got,
    pair_sum,
    rs_y,
    rs_x,
    rs_got,
    gathered,
    acc,
    term,
    term16,
    chunk,
    got_a,
    got_b,
    got_c,
    total,
    load_sem,
    pair_send,
    pair_recv,
    rs_send,
    rs_recv,
    sum_send,
    sum_recv,
    back_send,
    back_recv,
    out_send,
    out_recv,
    ag_send,
    ag_recv,
    diag_send,
    diag_recv,
    sib_send,
    sib_recv,
    ar_send,
    ar_recv,
):
    b = lax.axis_index("blk")
    d = lax.axis_index("dom")
    core = lax.rem(b, 2)
    chip = b // 2
    sibling = b + 1 - 2 * core
    column = chip // COL
    y = lax.rem(chip, COL)

    def chip_at(s):
        return lax.rem(column + s // COL, 2) * COL + lax.rem(y + lax.rem(s, COL), COL)

    def device_at(s):
        return 2 * chip_at(s) + core

    def remote(src, dst, send, recv, blk, dom):
        return pltpu.make_async_remote_copy(
            src_ref=src,
            dst_ref=dst,
            send_sem=send,
            recv_sem=recv,
            device_id=(blk, dom),
            device_id_type=MESH,
        )

    def await_bytes(ref, sem):
        pltpu.make_async_copy(ref, ref, sem).wait()

    def loop(lo, hi, body):
        def step(i, carry):
            body(i)
            return carry

        lax.fori_loop(lo, hi, step, 0)

    def block(i, n):
        return pl.ds(pl.multiple_of(i * n, n), n)

    loads = [
        pltpu.make_async_copy(src, dst, load_sem.at[i])
        for i, (src, dst) in enumerate(
            (
                (send_hbm, send_rows),
                (owner_hbm, owner_rows),
                (hw_hbm, hw_rows),
                (live_hbm, live_row),
                (feats_hbm, feats),
                (cot_hbm, cot),
                (tiles_hbm, tiles.at[:, pl.ds(1, TPG)]),
                (weight_hbm, weight),
            )
        )
    ]
    for load in loads:
        load.start()

    barrier = pltpu.get_barrier_semaphore()

    def greet_dom(k):
        pl.semaphore_signal(
            barrier, inc=1, device_id=(b, lax.rem(d + k, ND)), device_id_type=MESH
        )

    def greet_blk(k):
        pl.semaphore_signal(
            barrier, inc=1, device_id=(lax.rem(b + k, NB), d), device_id_type=MESH
        )

    loop(1, ND, greet_dom)
    loop(1, NB, greet_blk)

    for load in loads[:5]:
        load.wait()
    hw = hw_rows[...]
    hw_high = hw.astype(bf16)
    hw_low = (hw - hw_high.astype(f32)).astype(bf16)
    send = send_rows[...]
    owner = owner_rows[...]
    as_bf16 = lambda x: x.astype(f32).astype(bf16)
    stack = [as_bf16(send // 16), as_bf16(send % 16)]
    stack += [as_bf16(owner // 16), as_bf16(owner % 16), hw_high, hw_low]
    lane = lax.broadcasted_iota(jnp.int32, (SLOTS, LIST), 1)
    line = lax.broadcasted_iota(jnp.int32, (SLOTS, LIST), 0)
    spread = jnp.where(lane % SLOTS == line, 1.0, 0.0).astype(bf16)
    mine = lane // SLOTS == line

    def flat(x):
        return jnp.sum(jnp.where(mine, dot(x, spread), 0.0), axis=0, keepdims=True)

    rows = [flat(x) for x in stack]
    counts = jnp.broadcast_to(as_bf16(live_row[...]), (8, ND))
    count_row = dot(counts, jnp.where(mine, 1.0, 0.0).astype(bf16))[:1]
    slot = (lax.broadcasted_iota(jnp.int32, (1, LIST), 1) % SLOTS).astype(f32)
    send_row = jnp.where(slot < count_row, rows[0] * 16.0 + rows[1], -1.0)
    owner_row = rows[2] * 16.0 + rows[3]

    for i in range(PER):
        at = pl.ds(i * TILE, TILE)
        row = (lax.broadcasted_iota(jnp.int32, (TILE, LIST), 0) + i * TILE).astype(f32)
        pick[at, :] = jnp.where(row == send_row, 1.0, 0.0).astype(bf16)
    outgoing[...] = dot(pick[...], feats[...], 0, 0).astype(bf16)

    pl.semaphore_wait(barrier, ND + NB - 2)

    def ag_copy(s):
        return remote(
            feats, gathered.at[b], ag_send, ag_recv.at[s], device_at(s), d
        )

    def back_at(s):
        return lax.rem(column + s // COL, 2) * COL + lax.rem(y + COL - lax.rem(s, COL), COL)

    def sib_copy(s):
        at = gathered.at[2 * back_at(s) + core]
        return remote(at, at, sib_send, sib_recv.at[s], sibling, d)

    first, second = pl.ds(0, HALF), pl.ds(HALF, HALF)

    def diag_y(j):
        at = gathered.at[device_at(COL), first]
        return remote(at, at, diag_send, diag_recv.at[j], device_at(j), d)

    def diag_x(j):
        at = gathered.at[2 * back_at(j) + core, second]
        return remote(at, at, diag_send, diag_recv.at[COL + j], device_at(COL), d)

    ag_copy(COL).start()
    loop(1, COL, lambda s: ag_copy(s).start())
    remote(feats, gathered.at[b], sib_send, sib_recv.at[0], sibling, d).start()

    def dom_send(src, dst, send, recv):
        def body(i):
            half = i // 2
            k = half + 1 + lax.rem(i, 2) * (ND - 2 - 2 * half)
            q = lax.rem(d + k, ND)
            remote(
                src.at[block(q, SLOTS)], dst.at[block(d, SLOTS)], send, recv, b, q
            ).start()

        loop(0, ND - 1, body)

    dom_send(outgoing, incoming, out_send, out_recv)

    loads[5].wait()
    for i in range(PER):
        at = pl.ds(i * TILE, TILE)
        row = (lax.broadcasted_iota(jnp.int32, (TILE, LIST), 0) + i * TILE).astype(f32)
        hit = row == owner_row
        high[at, :] = jnp.where(hit, rows[4], 0.0).astype(bf16)
        low[at, :] = jnp.where(hit, rows[5], 0.0).astype(bf16)
    back[...] = (
        dot(high[...], cot[...], 0, 0) + dot(low[...], cot[...], 0, 0)
    ).astype(bf16)
    dom_send(back, returned, back_send, back_recv)

    zero = jnp.zeros((TILE, TILE), bf16)

    def clear(c):
        tiles[c, 0] = zero

    loop(0, NB, clear)
    loads[6].wait()

    def share(c):
        live = count_ref[c]
        spots = [jnp.where(t < live, pos_ref[t, 0, c], -1) for t in range(TPG)]
        for p in range(PER * PER):
            found = 0
            for t in range(TPG):
                found = jnp.where(spots[t] == p, t + 1, found)
            r, k = p // PER, p % PER
            adj[c, pl.ds(r * TILE, TILE), pl.ds(k * TILE, TILE)] = tiles[c, found]
        return dot(adj[c], cot[...], 0, 0).astype(bf16)

    def pair_copy(s):
        return remote(
            other.at[s], pair_got.at[s], pair_send, pair_recv.at[s], sibling, d
        )

    def other_step(i):
        s = lax.rem(i + COL + 1, CHIPS)
        other[s] = share(2 * chip_at(s) + 1 - core)
        pair_copy(s).start()

    loop(0, CHIPS, other_step)

    ag_copy(COL).wait_recv()
    loop(1, COL, lambda j: diag_y(j).start())
    sib_copy(COL).start()

    def column_step(s):
        ag_copy(s).wait_recv()
        diag_x(s).start()
        sib_copy(s).start()

    loop(1, COL, column_step)

    def own_step(i):
        s = lax.rem(i + COL + 1, CHIPS)
        own[s] = share(device_at(s))

    loop(0, CHIPS, own_step)

    def rs_first(j):
        return remote(
            pair_sum.at[COL + j, first], rs_y.at[j], rs_send, rs_recv.at[j], device_at(j), d
        )

    def rs_second(j):
        return remote(
            pair_sum.at[COL + j, second],
            rs_x.at[j],
            rs_send,
            rs_recv.at[COL + j],
            device_at(COL),
            d,
        )

    def sum_copy(s):
        return remote(
            pair_sum.at[s], rs_got.at[s], sum_send, sum_recv.at[s], device_at(s), d
        )

    def pair_step(s):
        pair_copy(s).wait_recv()
        pair_sum[s] = (own[s].astype(f32) + pair_got[s].astype(f32)).astype(bf16)

    def diag_step(j):
        pair_step(COL + j)
        rs_first(j).start()
        rs_second(j).start()

    loop(1, COL, diag_step)
    loop(1, COL + 1, pair_step)

    acc[...] = dot(adj[b], feats[...])

    def gain(at):
        acc[...] += dot(adj[at], gathered[at])

    loop(1, COL + 1, lambda s: gain(2 * back_at(s) + core))
    sib_copy(0).wait_recv()
    gain(sibling)

    def diag_wait(j):
        diag_y(j).wait_recv()
        diag_x(j).wait_recv()
        sib_copy(COL + j).start()
        gain(2 * back_at(COL + j) + core)

    loop(1, COL, diag_wait)

    def sib_step(s):
        sib_copy(s).wait_recv()
        gain(2 * back_at(s) + 1 - core)

    loop(1, CHIPS, sib_step)

    none = jnp.zeros((SLOTS, F), bf16)
    incoming[block(d, SLOTS), :] = none
    returned[block(d, SLOTS), :] = none
    others = pl.ds(0, LIST - SLOTS)
    await_bytes(incoming.at[others], out_recv)
    came = incoming[...]
    gained = (acc[...] + dot(high[...], came) + dot(low[...], came)).astype(bf16)
    whole = dot(gained, cot[...], 0, 0)
    term[...] = whole
    term16[...] = whole.astype(bf16)

    def blk_send(src_of, dst_of, stage):
        def body(k):
            to = lax.rem(b + k, NB)
            remote(
                src_of(to), dst_of(k), ar_send.at[stage], ar_recv.at[stage], to, d
            ).start()

        loop(1, NB, body)

    blk_send(lambda to: term16.at[block(to, PIECE)], lambda k: got_a.at[k], 0)
    loads[7].wait()
    layer_ref[...] = dot(gained, weight[...]).astype(bf16)

    await_bytes(got_a.at[pl.ds(1, NB - 1)], ar_recv.at[0])
    piece = term[block(b, PIECE), :]
    for k in range(1, NB):
        piece = piece + got_a[k].astype(f32)

    mine = lax.rem(d, NEAR)
    got_b[mine] = piece.astype(bf16)

    def near_send(k):
        to = d // NEAR * NEAR + lax.rem(mine + k, NEAR)
        at = got_b.at[mine]
        remote(at, at, ar_send.at[1], ar_recv.at[1], b, to).start()

    loop(1, NEAR, near_send)

    def column_sum(j):
        rs_second(j).wait_recv()
        at = pair_sum[j, HALF:].astype(f32) + rs_x[j].astype(f32)
        pair_sum[j, HALF:] = at.astype(bf16)
        sum_copy(j).start()

    def partner_sum(j):
        rs_first(j).wait_recv()

    loop(1, COL, partner_sum)
    both = pair_sum[COL, :HALF].astype(f32)
    for j in range(1, COL):
        both = both + rs_y[j].astype(f32)
    pair_sum[COL, :HALF] = both.astype(bf16)
    sum_copy(COL).start()
    loop(1, COL, column_sum)

    await_bytes(got_b.at[pl.ds(1, NEAR - 1)], ar_recv.at[1])
    piece = got_b[0].astype(f32)
    for k in range(1, NEAR):
        piece = piece + got_b[k].astype(f32)
    group = d // NEAR
    got_c[group] = piece.astype(bf16)

    def far_send(k):
        to = lax.rem(d + k * NEAR, ND)
        at = got_c.at[group]
        remote(at, at, ar_send.at[2], ar_recv.at[2], b, to).start()

    loop(1, FAR, far_send)
    pair_copy(0).wait_recv()
    acc[...] = own[0].astype(f32) + pair_got[0].astype(f32)
    await_bytes(got_c.at[pl.ds(1, FAR - 1)], ar_recv.at[2])
    piece = got_c[0].astype(f32)
    for k in range(1, FAR):
        piece = piece + got_c[k].astype(f32)
    piece = (piece * (float(NB * ND * ROWS) ** -0.5)).astype(bf16)
    chunk[...] = piece
    blk_send(lambda to: chunk, lambda k: total.at[block(b, PIECE)], 3)
    total[block(b, PIECE), :] = piece
    await_bytes(returned.at[others], back_recv)
    acc[...] += dot(pick[...], returned[...])

    def sum_step(s):
        sum_copy(s).wait_recv()
        acc[...] += rs_got[s].astype(f32)

    loop(1, COL + 1, sum_step)
    fgrad_ref[...] = dot(acc[...].astype(bf16), weight[...], 1, 1).astype(bf16)
    await_bytes(total.at[pl.ds(0, F - PIECE)], ar_recv.at[3])
    wgrad_ref[...] = total[...].astype(f32)

    await_bytes(pair_got, pair_send)
    await_bytes(pair_sum.at[pl.ds(0, COL - 1)], rs_send)
    await_bytes(pair_sum.at[pl.ds(0, COL)], sum_send)
    await_bytes(returned.at[others], back_send)
    await_bytes(incoming.at[others], out_send)
    await_bytes(pair_sum.at[pl.ds(0, COL)], ag_send)
    await_bytes(pair_sum.at[pl.ds(0, COL - 1)], diag_send)
    await_bytes(pair_sum, sib_send)
    await_bytes(got_a.at[pl.ds(1, NB - 1)], ar_send.at[0])
    await_bytes(got_b.at[pl.ds(1, NEAR - 1)], ar_send.at[1])
    await_bytes(got_c.at[pl.ds(1, FAR - 1)], ar_send.at[2])
    await_bytes(got_a.at[pl.ds(1, NB - 1)], ar_send.at[3])


def mesh_part(pos, count, tiles, feats, cot, weight, send, live, owner, hw):
    shape = jax.ShapeDtypeStruct
    far = pl.BlockSpec(memory_space=pltpu.HBM)
    near = pl.BlockSpec(memory_space=pltpu.VMEM)
    scalar = pl.BlockSpec(memory_space=pltpu.SMEM)
    dma = pltpu.SemaphoreType.DMA
    vmem = pltpu.VMEM
    return pl.pallas_call(
        mesh_kernel,
        out_shape=[
            shape((ROWS, F), bf16),
            shape((ROWS, F), bf16),
            shape((F, F), f32),
        ],
        in_specs=[scalar] * 2 + [far] * 8,
        out_specs=[near] * 3,
        scratch_shapes=[
            vmem((NB, TPG + 1, TILE, TILE), bf16),
            vmem((ROWS, F), bf16),
            vmem((ROWS, F), bf16),
            vmem((F, F), bf16),
            vmem((ND, SLOTS), jnp.int32),
            vmem((ND, SLOTS), jnp.int32),
            vmem((ND, SLOTS), f32),
            vmem((1, ND), jnp.int32),
            vmem((NB, ROWS, ROWS), bf16),
            vmem((ROWS, LIST), bf16),
            vmem((ROWS, LIST), bf16),
            vmem((ROWS, LIST), bf16),
            vmem((LIST, F), bf16),
            vmem((LIST, F), bf16),
            vmem((LIST, F), bf16),
            vmem((LIST, F), bf16),
            vmem((CHIPS, ROWS, F), bf16),
            vmem((CHIPS, ROWS, F), bf16),
            vmem((CHIPS, ROWS, F), bf16),
            vmem((CHIPS, ROWS, F), bf16),
            vmem((COL, HALF, F), bf16),
            vmem((COL, HALF, F), bf16),
            vmem((COL + 1, ROWS, F), bf16),
            vmem((NB, ROWS, F), bf16),
            vmem((ROWS, F), f32),
            vmem((F, F), f32),
            vmem((F, F), bf16),
            vmem((PIECE, F), bf16),
            vmem((NB, PIECE, F), bf16),
            vmem((NEAR, PIECE, F), bf16),
            vmem((FAR, PIECE, F), bf16),
            vmem((F, F), bf16),
            dma((8,)),
            dma,
            dma((CHIPS,)),
            dma,
            dma((CHIPS,)),
            dma,
            dma((COL + 1,)),
            dma,
            dma,
            dma,
            dma,
            dma,
            dma((COL + 1,)),
            dma,
            dma((CHIPS,)),
            dma,
            dma((CHIPS,)),
            dma((4,)),
            dma((4,)),
        ],
        compiler_params=pltpu.CompilerParams(
            collective_id=0, has_side_effects=True, vmem_limit_bytes=60 * MIB
        ),
    )(pos, count, tiles, feats, cot, weight, send, live, owner, hw)


def final_kernel(*refs):
    sources, targets, held, (load_sem, store_sem) = (
        refs[:3],
        refs[3:6],
        refs[6:9],
        refs[9:],
    )
    loads = [
        pltpu.make_async_copy(src, at, load_sem.at[i])
        for i, (src, at) in enumerate(zip(sources, held))
    ]
    stores = [
        pltpu.make_async_copy(at, dst, store_sem.at[i])
        for i, (at, dst) in enumerate(zip(held, targets))
    ]
    for load in loads:
        load.start()
    for load, store in zip(loads, stores):
        load.wait()
        store.start()
    for store in stores:
        store.wait()


def final_part(*results):
    far = pl.BlockSpec(memory_space=pltpu.HBM)
    return pl.pallas_call(
        final_kernel,
        out_shape=[jax.ShapeDtypeStruct(x.shape, x.dtype) for x in results],
        in_specs=[far] * 3,
        out_specs=[far] * 3,
        scratch_shapes=[pltpu.VMEM(x.shape, x.dtype) for x in results]
        + [pltpu.SemaphoreType.DMA((3,))] * 2,
        compiler_params=pltpu.CompilerParams(vmem_limit_bytes=60 * MIB),
    )(*results)


def on_device(
    features,
    weight,
    tiles,
    tile_pos,
    tile_count,
    send_list,
    send_count,
    owner_map,
    halo_weight,
    cotangent,
):
    results = mesh_part(
        jnp.transpose(tile_pos, (0, 3, 1, 2))[0],
        tile_count[0, 0],
        tiles[0, 0],
        features[0],
        cotangent[0],
        weight,
        send_list[0, 0],
        send_count[0],
        owner_map[0, 0],
        halo_weight[0, 0],
    )
    layer_out, feature_grad, weight_grad = final_part(*results)
    return (layer_out[None], feature_grad[None], weight_grad)


def solution(mesh):
    return jax.shard_map(
        on_device,
        mesh=mesh,
        in_specs=(
            P("dom", "blk", None),
            P(),
            P("dom", "blk", None, None, None, None),
            P("dom", "blk", None, None),
            P("dom", "blk", None),
            P("dom", "blk", None, None),
            P("dom", "blk", None),
            P("dom", "blk", None, None),
            P("dom", "blk", None, None),
            P("dom", "blk", None),
        ),
        out_specs=(P("dom", "blk", None), P("dom", "blk", None), P()),
        check_vma=False,
    )
```

time: 138 us -> 81.6 us (0.59)
  Pallas kernels: 122 us -> 80.8 us
  local copies, waits for them, and re-layouts: 14.6 us -> 0 us
    pallas_call x1, Pallas kernels: 110 us -> 78.9 us  [mesh_part(): pl.pallas_call(mesh_kernel, out_shape=[shape((ROWS, F), bf16), shape((ROW...]
    unnamed x20 -> x0, local copies, waits for them, and re-layouts: 12 us -> none
    pallas_call x1, Pallas kernels: 11.2 us -> 1.88 us  [final_part(): pl.pallas_call(final_kernel, out_shape=[jax.ShapeDtypeStruct(x.shape, x.d...]
    reshape x3 -> x0, local copies, waits for them, and re-layouts: 1.68 us -> none  [the longest x1 0.8 us: on_device(): owner_map.reshape(1, LIST)]
where the time goes in v2:
time: 81.6 us; the launch traced here: 81.4 us
  Pallas kernels  80.8 us (99%)
    pallas_call x1, Pallas kernels, mesh_part(): pl.pallas_call(mesh_kernel, out_shape=[shape((ROWS, F), bf16), shape((ROW...  78.9 us
    pallas_call x1, Pallas kernels, final_part(): pl.pallas_call(final_kernel, out_shape=[jax.ShapeDtypeStruct(x.shape, x.d...  1.88 us

profile of v2, /device:TPU:1, one launch (start us, length us, event | category | flops | bytes accessed | tf_op | source)
XLA Modules:
  0.0 81.4 jit_solution(14576481713994485600)
XLA Ops:
  0.6 78.9 %shard_map.121 = (bf16[512,256]{1,0:T(8,128)(2,1)}, bf16[512,256]{1,0:T(8,128)(2,1)}, f32[256,256]{1,0:T(8,128)}) custom-call(s32[6,1,16]{2,1,0:T(1,128)} %bitcast.19, s32[16]{0:T(128)} %bitcast.20, bf16[16,6,128,128]{3,2,1,0:T(8,128)(2,1)} %bitcast.13, bf16[512,256]{1,0:T(8,128)(2,1)} %bitcast.14, bf16[512,256]{1,0:T(8,128)(2,1)} %bitcast.15, ...), custom_call_target="tpu_custom_call" | custom-call | tf_op jit(solution)/shard_map/pallas_call | solution.py:471
  79.5 1.9 %shard_map.122 = (bf16[512,256]{1,0:T(8,128)(2,1)}, bf16[512,256]{1,0:T(8,128)(2,1)}, f32[256,256]{1,0:T(8,128)}) custom-call(bf16[512,256]{1,0:T(8,128)(2,1)} %get-tuple-element.9.refs_0_, bf16[512,256]{1,0:T(8,128)(2,1)} %get-tuple-element.10.refs_1_, f32[256,256]{1,0:T(8,128)} %get-tuple-element.11.refs_2_), custom_call_target="tpu_custom_call" | custom-call | tf_op jit(solution)/shard_map/pallas_call | solution.py:565

commit v3 on v2

--- a/solution.py
+++ b/solution.py
@@ -21,8 +21,8 @@
 SLOTS = 32
 LIST = ND * SLOTS
 PIECE = F // NB
-NEAR = 8
-FAR = ND // NEAR
+PLANE = 2 * NB
+RING = ND // 2
 MIB = 1 << 20
 
 bf16 = jnp.bfloat16
@@ -76,8 +76,7 @@
     term16,
     chunk,
     got_a,
-    got_b,
-    got_c,
+    got_z,
     total,
     load_sem,
     pair_send,
@@ -92,6 +91,7 @@
     out_recv,
     ag_send,
     ag_recv,
+    rest_recv,
     diag_send,
     diag_recv,
     sib_send,
@@ -202,9 +202,18 @@
 
     pl.semaphore_wait(barrier, ND + NB - 2)
 
-    def ag_copy(s):
+    first, second = pl.ds(0, HALF), pl.ds(HALF, HALF)
+
+    def lead_copy(s, half):
+        at = gathered.at[b, half]
         return remote(
-            feats, gathered.at[b], ag_send, ag_recv.at[s], device_at(s), d
+            feats.at[half], at, ag_send, ag_recv.at[s], device_at(s), d
+        )
+
+    def rest_copy(s, half):
+        at = gathered.at[b, half]
+        return remote(
+            feats.at[half], at, ag_send, rest_recv.at[s], device_at(s), d
         )
 
     def back_at(s):
@@ -214,8 +223,6 @@
         at = gathered.at[2 * back_at(s) + core]
         return remote(at, at, sib_send, sib_recv.at[s], sibling, d)
 
-    first, second = pl.ds(0, HALF), pl.ds(HALF, HALF)
-
     def diag_y(j):
         at = gathered.at[device_at(COL), first]
         return remote(at, at, diag_send, diag_recv.at[j], device_at(j), d)
@@ -224,9 +231,30 @@
         at = gathered.at[2 * back_at(j) + core, second]
         return remote(at, at, diag_send, diag_recv.at[COL + j], device_at(COL), d)
 
-    ag_copy(COL).start()
-    loop(1, COL, lambda s: ag_copy(s).start())
+    lead_copy(COL, first).start()
+    for j in (1, 3, 2):
+        lead_copy(j, second).start()
+    rest_copy(COL, second).start()
+    for j in (1, 3, 2):
+        rest_copy(j, first).start()
     remote(feats, gathered.at[b], sib_send, sib_recv.at[0], sibling, d).start()
+
+    def back_copy(k):
+        q = lax.rem(d + k, ND)
+        remote(
+            back.at[block(q, SLOTS)],
+            returned.at[block(d, SLOTS)],
+            back_send,
+            back_recv,
+            b,
+            q,
+        ).start()
+
+    def odd(i):
+        back_copy(i + 1 + lax.rem(i, 2) * (ND - 1 - 2 * i))
+
+    def even(i):
+        back_copy(i + 2 + lax.rem(i, 2) * (ND - 3 - 2 * i))
 
     def dom_send(src, dst, send, recv):
         def body(i):
@@ -251,7 +279,15 @@
     back[...] = (
         dot(high[...], cot[...], 0, 0) + dot(low[...], cot[...], 0, 0)
     ).astype(bf16)
-    dom_send(back, returned, back_send, back_recv)
+    loop(0, ND // 2, odd)
+    loop(0, 8, even)
+
+    lead_copy(COL, first).wait_recv()
+    for j in (1, 3, 2):
+        diag_y(j).start()
+    for j in (1, 3, 2):
+        lead_copy(j, second).wait_recv()
+        diag_x(j).start()
 
     zero = jnp.zeros((TILE, TILE), bf16)
 
@@ -284,16 +320,11 @@
 
     loop(0, CHIPS, other_step)
 
-    ag_copy(COL).wait_recv()
-    loop(1, COL, lambda j: diag_y(j).start())
-    sib_copy(COL).start()
-
-    def column_step(s):
-        ag_copy(s).wait_recv()
-        diag_x(s).start()
+    def whole_step(s):
+        rest_copy(s, first).wait_recv()
         sib_copy(s).start()
 
-    loop(1, COL, column_step)
+    loop(1, COL + 1, whole_step)
 
     def own_step(i):
         s = lax.rem(i + COL + 1, CHIPS)
@@ -364,36 +395,48 @@
     came = incoming[...]
     gained = (acc[...] + dot(high[...], came) + dot(low[...], came)).astype(bf16)
     whole = dot(gained, cot[...], 0, 0)
-    term[...] = whole
-    term16[...] = whole.astype(bf16)
-
-    def blk_send(src_of, dst_of, stage):
-        def body(k):
-            to = lax.rem(b + k, NB)
+    side = lax.rem(d, 2)
+    for i in range(2):
+        half = whole[:, i * TILE : (i + 1) * TILE].reshape(NB, PIECE, TILE)
+        term[i * NB : (i + 1) * NB] = half
+        term16[i * NB : (i + 1) * NB] = half.astype(bf16)
+
+    def plane_send(src_of, dst_of, stage):
+        def body(n):
+            flip = n // NB
+            to = lax.rem(b + n, NB)
+            to_side = lax.rem(side + flip, 2)
             remote(
-                src_of(to), dst_of(k), ar_send.at[stage], ar_recv.at[stage], to, d
+                src_of(to_side * NB + to),
+                dst_of(n),
+                ar_send.at[stage],
+                ar_recv.at[stage],
+                to,
+                d - side + to_side,
             ).start()
 
-        loop(1, NB, body)
-
-    blk_send(lambda to: term16.at[block(to, PIECE)], lambda k: got_a.at[k], 0)
+        loop(1, PLANE, body)
+
+    place = side * NB + b
+    plane_send(lambda n: term16.at[n], lambda n: got_a.at[n], 0)
     loads[7].wait()
     layer_ref[...] = dot(gained, weight[...]).astype(bf16)
 
-    await_bytes(got_a.at[pl.ds(1, NB - 1)], ar_recv.at[0])
-    piece = term[block(b, PIECE), :]
-    for k in range(1, NB):
-        piece = piece + got_a[k].astype(f32)
-
-    mine = lax.rem(d, NEAR)
-    got_b[mine] = piece.astype(bf16)
-
-    def near_send(k):
-        to = d // NEAR * NEAR + lax.rem(mine + k, NEAR)
-        at = got_b.at[mine]
+    await_bytes(got_a.at[pl.ds(1, PLANE - 1)], ar_recv.at[0])
+    piece = term[place]
+    for n in range(1, PLANE):
+        piece = piece + got_a[n].astype(f32)
+
+    z = d // 2
+    got_z[z] = piece.astype(bf16)
+
+    def ring_send(k):
+        at = got_z.at[z]
+        to = lax.rem(d + 2 * k, ND)
         remote(at, at, ar_send.at[1], ar_recv.at[1], b, to).start()
 
-    loop(1, NEAR, near_send)
+    loop(1, RING, ring_send)
+    loop(8, ND // 2 - 1, even)
 
     def column_sum(j):
         rs_second(j).wait_recv()
@@ -412,29 +455,16 @@
     sum_copy(COL).start()
     loop(1, COL, column_sum)
 
-    await_bytes(got_b.at[pl.ds(1, NEAR - 1)], ar_recv.at[1])
-    piece = got_b[0].astype(f32)
-    for k in range(1, NEAR):
-        piece = piece + got_b[k].astype(f32)
-    group = d // NEAR
-    got_c[group] = piece.astype(bf16)
-
-    def far_send(k):
-        to = lax.rem(d + k * NEAR, ND)
-        at = got_c.at[group]
-        remote(at, at, ar_send.at[2], ar_recv.at[2], b, to).start()
-
-    loop(1, FAR, far_send)
     pair_copy(0).wait_recv()
     acc[...] = own[0].astype(f32) + pair_got[0].astype(f32)
-    await_bytes(got_c.at[pl.ds(1, FAR - 1)], ar_recv.at[2])
-    piece = got_c[0].astype(f32)
-    for k in range(1, FAR):
-        piece = piece + got_c[k].astype(f32)
+    await_bytes(got_z.at[pl.ds(1, RING - 1)], ar_recv.at[1])
+    piece = got_z[0].astype(f32)
+    for k in range(1, RING):
+        piece = piece + got_z[k].astype(f32)
     piece = (piece * (float(NB * ND * ROWS) ** -0.5)).astype(bf16)
     chunk[...] = piece
-    blk_send(lambda to: chunk, lambda k: total.at[block(b, PIECE)], 3)
-    total[block(b, PIECE), :] = piece
+    plane_send(lambda n: chunk, lambda n: total.at[place], 2)
+    total[place] = piece
     await_bytes(returned.at[others], back_recv)
     acc[...] += dot(pick[...], returned[...])
 
@@ -444,8 +474,10 @@
 
     loop(1, COL + 1, sum_step)
     fgrad_ref[...] = dot(acc[...].astype(bf16), weight[...], 1, 1).astype(bf16)
-    await_bytes(total.at[pl.ds(0, F - PIECE)], ar_recv.at[3])
-    wgrad_ref[...] = total[...].astype(f32)
+    await_bytes(total.at[pl.ds(0, PLANE - 1)], ar_recv.at[2])
+    for i in range(2):
+        half = total[i * NB : (i + 1) * NB].astype(f32).reshape(F, TILE)
+        wgrad_ref[:, i * TILE : (i + 1) * TILE] = half
 
     await_bytes(pair_got, pair_send)
     await_bytes(pair_sum.at[pl.ds(0, COL - 1)], rs_send)
@@ -455,10 +487,9 @@
     await_bytes(pair_sum.at[pl.ds(0, COL)], ag_send)
     await_bytes(pair_sum.at[pl.ds(0, COL - 1)], diag_send)
     await_bytes(pair_sum, sib_send)
-    await_bytes(got_a.at[pl.ds(1, NB - 1)], ar_send.at[0])
-    await_bytes(got_b.at[pl.ds(1, NEAR - 1)], ar_send.at[1])
-    await_bytes(got_c.at[pl.ds(1, FAR - 1)], ar_send.at[2])
-    await_bytes(got_a.at[pl.ds(1, NB - 1)], ar_send.at[3])
+    await_bytes(got_a.at[pl.ds(1, PLANE - 1)], ar_send.at[0])
+    await_bytes(got_z.at[pl.ds(1, RING - 1)], ar_send.at[1])
+    await_bytes(got_a.at[pl.ds(1, PLANE - 1)], ar_send.at[2])
 
 
 def mesh_part(pos, count, tiles, feats, cot, weight, send, live, owner, hw):
@@ -503,13 +534,12 @@
             vmem((COL + 1, ROWS, F), bf16),
             vmem((NB, ROWS, F), bf16),
             vmem((ROWS, F), f32),
-            vmem((F, F), f32),
-            vmem((F, F), bf16),
-            vmem((PIECE, F), bf16),
-            vmem((NB, PIECE, F), bf16),
-            vmem((NEAR, PIECE, F), bf16),
-            vmem((FAR, PIECE, F), bf16),
-            vmem((F, F), bf16),
+            vmem((PLANE, PIECE, TILE), f32),
+            vmem((PLANE, PIECE, TILE), bf16),
+            vmem((PIECE, TILE), bf16),
+            vmem((PLANE, PIECE, TILE), bf16),
+            vmem((RING, PIECE, TILE), bf16),
+            vmem((PLANE, PIECE, TILE), bf16),
             dma((8,)),
             dma,
             dma((CHIPS,)),
@@ -523,12 +553,13 @@
             dma,
             dma,
             dma((COL + 1,)),
+            dma((COL + 1,)),
             dma,
             dma((CHIPS,)),
             dma,
             dma((CHIPS,)),
-            dma((4,)),
-            dma((4,)),
+            dma((3,)),
+            dma((3,)),
         ],
         compiler_params=pltpu.CompilerParams(
             collective_id=0, has_side_effects=True, vmem_limit_bytes=60 * MIB

time: 81.6 us -> 77.2 us (0.946)
  Pallas kernels: 80.8 us -> 76.3 us
    pallas_call x1, Pallas kernels: 78.9 us -> 74.5 us  [mesh_part(): pl.pallas_call(mesh_kernel, out_shape=[shape((ROWS, F), bf16), shape((ROW...]
where the time goes in v3:
time: 77.2 us; the launch traced here: 77 us
  Pallas kernels  76.3 us (99%)
    pallas_call x1, Pallas kernels, mesh_part(): pl.pallas_call(mesh_kernel, out_shape=[shape((ROWS, F), bf16), shape((ROW...  74.5 us
    pallas_call x1, Pallas kernels, final_part(): pl.pallas_call(final_kernel, out_shape=[jax.ShapeDtypeStruct(x.shape, x.d...  1.88 us

profile of v3, /device:TPU:1, one launch (start us, length us, event | category | flops | bytes accessed | tf_op | source)
XLA Modules:
  0.0 77.0 jit_solution(3342775291114200550)
XLA Ops:
  0.6 74.5 %shard_map.121 = (bf16[512,256]{1,0:T(8,128)(2,1)}, bf16[512,256]{1,0:T(8,128)(2,1)}, f32[256,256]{1,0:T(8,128)}) custom-call(s32[6,1,16]{2,1,0:T(1,128)} %bitcast.19, s32[16]{0:T(128)} %bitcast.20, bf16[16,6,128,128]{3,2,1,0:T(8,128)(2,1)} %bitcast.13, bf16[512,256]{1,0:T(8,128)(2,1)} %bitcast.14, bf16[512,256]{1,0:T(8,128)(2,1)} %bitcast.15, ...), custom_call_target="tpu_custom_call" | custom-call | tf_op jit(solution)/shard_map/pallas_call | solution.py:502
  75.1 1.9 %shard_map.122 = (bf16[512,256]{1,0:T(8,128)(2,1)}, bf16[512,256]{1,0:T(8,128)(2,1)}, f32[256,256]{1,0:T(8,128)}) custom-call(bf16[512,256]{1,0:T(8,128)(2,1)} %get-tuple-element.9.refs_0_, bf16[512,256]{1,0:T(8,128)(2,1)} %get-tuple-element.10.refs_1_, f32[256,256]{1,0:T(8,128)} %get-tuple-element.11.refs_2_), custom_call_target="tpu_custom_call" | custom-call | tf_op jit(solution)/shard_map/pallas_call | solution.py:596

commit v4 on v3

--- a/solution.py
+++ b/solution.py
@@ -297,7 +297,7 @@
     loop(0, NB, clear)
     loads[6].wait()
 
-    def share(c):
+    def build(c):
         live = count_ref[c]
         spots = [jnp.where(t < live, pos_ref[t, 0, c], -1) for t in range(TPG)]
         for p in range(PER * PER):
@@ -306,6 +306,8 @@
                 found = jnp.where(spots[t] == p, t + 1, found)
             r, k = p // PER, p % PER
             adj[c, pl.ds(r * TILE, TILE), pl.ds(k * TILE, TILE)] = tiles[c, found]
+
+    def share(c):
         return dot(adj[c], cot[...], 0, 0).astype(bf16)
 
     def pair_copy(s):
@@ -315,7 +317,9 @@
 
     def other_step(i):
         s = lax.rem(i + COL + 1, CHIPS)
-        other[s] = share(2 * chip_at(s) + 1 - core)
+        c = 2 * chip_at(s) + 1 - core
+        build(c)
+        other[s] = share(c)
         pair_copy(s).start()
 
     loop(0, CHIPS, other_step)
@@ -330,7 +334,7 @@
         s = lax.rem(i + COL + 1, CHIPS)
         own[s] = share(device_at(s))
 
-    loop(0, CHIPS, own_step)
+    loop(0, NB // 2, lambda i: build(2 * i + core))
 
     def rs_first(j):
         return remote(
@@ -361,8 +365,6 @@
         rs_first(j).start()
         rs_second(j).start()
 
-    loop(1, COL, diag_step)
-    loop(1, COL + 1, pair_step)
 
     acc[...] = dot(adj[b], feats[...])
 
@@ -422,6 +424,9 @@
     loads[7].wait()
     layer_ref[...] = dot(gained, weight[...]).astype(bf16)
 
+    loop(0, CHIPS, own_step)
+    loop(1, COL, diag_step)
+    loop(1, COL + 1, pair_step)
     await_bytes(got_a.at[pl.ds(1, PLANE - 1)], ar_recv.at[0])
     piece = term[place]
     for n in range(1, PLANE):

time: 77.2 us -> 76.4 us (0.990)
  no operation moved by 1% of the time
where the time goes in v4:
time: 76.4 us; the launch traced here: 76.3 us
  Pallas kernels  75.6 us (99%)
    pallas_call x1, Pallas kernels, mesh_part(): pl.pallas_call(mesh_kernel, out_shape=[shape((ROWS, F), bf16), shape((ROW...  73.7 us
    pallas_call x1, Pallas kernels, final_part(): pl.pallas_call(final_kernel, out_shape=[jax.ShapeDtypeStruct(x.shape, x.d...  1.88 us

profile of v4, /device:TPU:1, one launch (start us, length us, event | category | flops | bytes accessed | tf_op | source)
XLA Modules:
  0.0 76.3 jit_solution(5126553828184515408)
XLA Ops:
  0.6 73.7 %shard_map.121 = (bf16[512,256]{1,0:T(8,128)(2,1)}, bf16[512,256]{1,0:T(8,128)(2,1)}, f32[256,256]{1,0:T(8,128)}) custom-call(s32[6,1,16]{2,1,0:T(1,128)} %bitcast.19, s32[16]{0:T(128)} %bitcast.20, bf16[16,6,128,128]{3,2,1,0:T(8,128)(2,1)} %bitcast.13, bf16[512,256]{1,0:T(8,128)(2,1)} %bitcast.14, bf16[512,256]{1,0:T(8,128)(2,1)} %bitcast.15, ...), custom_call_target="tpu_custom_call" | custom-call | tf_op jit(solution)/shard_map/pallas_call | solution.py:507
  74.4 1.9 %shard_map.122 = (bf16[512,256]{1,0:T(8,128)(2,1)}, bf16[512,256]{1,0:T(8,128)(2,1)}, f32[256,256]{1,0:T(8,128)}) custom-call(bf16[512,256]{1,0:T(8,128)(2,1)} %get-tuple-element.9.refs_0_, bf16[512,256]{1,0:T(8,128)(2,1)} %get-tuple-element.10.refs_1_, f32[256,256]{1,0:T(8,128)} %get-tuple-element.11.refs_2_), custom_call_target="tpu_custom_call" | custom-call | tf_op jit(solution)/shard_map/pallas_call | solution.py:601
